TPU v7x, 32 devices: a whole 2x2x4 slice. The times are simulated.
32 devices in a mesh: fsdp: 4 (over z), ep: 8 (over y, x, core).
Axes of the slice: x: 2, y: 2, z: 4, core: 2. Of those that a mesh axis runs over, the one named last changes fastest.
Arguments:
- deltas: bfloat16 [8, 7168, 2048], P('ep', 'fsdp')
- sketch_matrix: bfloat16 [2048, 256], replicated, may hold values from -0.125 to 0.125
- owner_of: int32 [8], replicated, may hold values from 0 to 7, as said below
- serving: bfloat16 [16, 7168, 2048], P('ep', 'fsdp'), may hold values from -4 to 4
Outputs:
- updated: bfloat16 [16, 7168, 2048], P('ep', 'fsdp')
Inputs may be any that keep to these rules, and one draw needn't show every extreme that they name: `owner_of`: each of the 8 owners owns at most 2 experts; in every draw some owner owns exactly 2 and some own none.
All inputs are finite; a program needn't handle non-finite values.
Results may differ from a plain program's by a relative error of at most 0.007.
Values may be sent and summed in bfloat16 or wider, within the bound.
A program may use at most 128 MiB of HBM per device.

v0:
```python
import functools

import jax
import jax.numpy as jnp
from jax import lax
from jax.experimental import pallas as pl
from jax.experimental.pallas import tpu as pltpu
from jax.sharding import PartitionSpec as P

D = 7168
POWER = 2
MESH = pl.DeviceIdType.MESH
CHUNK = 128
VMEM_LIMIT = 56 * 1024 * 1024
F32 = jnp.float32
BF16 = jnp.bfloat16


def flip(me, bits):
    for bit in bits:
        me = me + (1 - 2 * lax.rem(lax.div(me, 1 << bit), 2)) * (1 << bit)
    return me


def digits(count):
    return list(range(count.bit_length() - 1))


def greet(me, n, own=None, bits=()):
    barrier = pltpu.get_barrier_semaphore()
    for bit in bits:
        pl.semaphore_signal(barrier, inc=1, device_id={"ep": flip(own, [bit])}, device_id_type=MESH)
    peers = len(bits)
    if n > 0:
        @pl.when(me > 0)
        def _():
            pl.semaphore_signal(barrier, inc=1, device_id={"fsdp": me - 1}, device_id_type=MESH)

        @pl.when(me < n - 1)
        def _():
            pl.semaphore_signal(barrier, inc=1, device_id={"fsdp": me + 1}, device_id_type=MESH)

        peers = peers + (me > 0).astype(jnp.int32) + (me < n - 1).astype(jnp.int32)
    pl.semaphore_wait(barrier, peers)


class Cube:
    def __init__(self, own, order, at, ssem, rsem):
        self.own, self.order, self.at, self.ssem, self.rsem = own, order, at, ssem, rsem

    def copy(self, held, bit, index):
        block = self.at(lax.div(flip(self.own, held), 2))
        return pltpu.make_async_remote_copy(
            src_ref=block, dst_ref=block, send_sem=self.ssem.at[index], recv_sem=self.rsem.at[index],
            device_id={"ep": flip(self.own, [bit])}, device_id_type=MESH)

    def across(self, stage):
        sets = [[]]
        for bit in self.order[:stage]:
            sets = sets + [one + [bit] for one in sets]
        return [(one, self.order[stage], (1 << stage) - 1 + i) for i, one in enumerate(sets)]

    def run(self, stage):
        if stage > 0:
            for one, bit, index in self.across(stage - 1):
                self.copy(one + [bit], bit, index).wait_recv()
        if stage < len(self.order):
            for plan in self.across(stage):
                self.copy(*plan).start()

    def finish(self):
        for stage in range(len(self.order)):
            for plan in self.across(stage):
                self.copy(*plan).wait_send()


def cubes(own, count, ref, ssem, rsem):
    inner = digits(count)[1:]
    half = ref.shape[1] // 2
    return [
        Cube(own, order, lambda e, h=h: ref.at[e, pl.ds(h * half, half)], ssem.at[h], rsem.at[h])
        for h, order in enumerate((inner, inner[::-1]))
    ]


def moves(me, n, part, bufs, ssem, rsem):
    send_r, send_l, recv_l, recv_r = bufs
    def to_right(j):
        return pltpu.make_async_remote_copy(
            src_ref=send_r.at[j], dst_ref=recv_l.at[j], send_sem=ssem.at[0, j],
            recv_sem=rsem.at[0, j], device_id={"fsdp": jnp.minimum(me + 1, n - 1)}, device_id_type=MESH)

    def to_left(j):
        return pltpu.make_async_remote_copy(
            src_ref=send_l.at[j], dst_ref=recv_r.at[j], send_sem=ssem.at[1, j],
            recv_sem=rsem.at[1, j], device_id={"fsdp": jnp.maximum(me - 1, 0)}, device_id_type=MESH)

    @pl.when(me == 0)
    def _():
        recv_l[...] = jnp.zeros_like(recv_l)

    @pl.when(me == n - 1)
    def _():
        recv_r[...] = jnp.zeros_like(recv_r)

    def rightward(j):
        @pl.when(me > 0)
        def _():
            to_right(j).wait_recv()

        @pl.when(me < n - 1)
        def _():
            send_r[j] = (part[j] + recv_l[j].astype(F32)).astype(send_r.dtype)
            to_right(j).start()

    def leftward(j):
        @pl.when(me < n - 1)
        def _():
            to_left(j).wait_recv()

        @pl.when(me > 0)
        def _():
            send_l[j] = (part[j] + recv_r[j].astype(F32)).astype(send_l.dtype)
            to_left(j).start()

    def total(j):
        return part[j] + recv_l[j].astype(F32) + recv_r[j].astype(F32)

    def drain(j, carry):
        @pl.when(me < n - 1)
        def _():
            to_right(j).wait_send()

        @pl.when(me > 0)
        def _():
            to_left(j).wait_send()

        return carry

    return rightward, leftward, total, drain


def chain_sum(me, n, chunks, part, compute, emit, bufs, ssem, rsem, first=None):
    lower = me < n // 2
    edge = jnp.minimum(me, n - 1 - me)
    skew = jnp.where(edge == 0, chunks, jnp.minimum(n - 2 * edge, chunks))
    rightward, leftward, total, drain = moves(me, n, part, bufs, ssem, rsem)
    if first is not None:
        fpart, fcompute, femit, fbufs, fssem, frsem = first
        frightward, fleftward, ftotal, fdrain = moves(me, n, fpart, fbufs, fssem, frsem)

    def step(t, carry):
        if first is not None:
            @pl.when(t == 0)
            def _():
                fpart[0] = fcompute()

                @pl.when(lower)
                def _():
                    frightward(0)

                @pl.when(jnp.logical_not(lower))
                def _():
                    fleftward(0)

            @pl.when(t == skew)
            def _():
                @pl.when(lower)
                def _():
                    fleftward(0)

                @pl.when(jnp.logical_not(lower))
                def _():
                    frightward(0)

                femit(ftotal(0))

        @pl.when(t < chunks)
        def _():
            part[t] = compute(t)

            @pl.when(lower)
            def _():
                rightward(t)

            @pl.when(jnp.logical_not(lower))
            def _():
                leftward(t)

        @pl.when((t >= skew) & (t < skew + chunks))
        def _():
            j = t - skew

            @pl.when(lower)
            def _():
                leftward(j)

            @pl.when(jnp.logical_not(lower))
            def _():
                rightward(j)

            emit(j, total(j))

        return carry

    lax.fori_loop(0, 2 * chunks, step, 0)

    lax.fori_loop(0, chunks, drain, 0)
    if first is not None:
        fdrain(0, 0)


def power_kernel(n, tile, chunks, a_ref, w_ref, y_ref, yt, p, part, send_r, send_l, recv_l, recv_r, ssem, rsem):
    me = lax.axis_index("fsdp")
    rows = a_ref.shape[0]
    greet(me, n)

    def sketch(weights):
        def body(i, carry):
            at = pl.ds(pl.multiple_of(i * tile, tile), tile)
            block = jnp.dot(a_ref[at, :], weights[...], preferred_element_type=F32)
            y_ref[at, :] = block.astype(BF16)
            yt[:, at] = block.T.astype(BF16)
            return carry

        lax.fori_loop(0, rows // tile, body, 0)

    def compute(j):
        at = pl.ds(pl.multiple_of(j * CHUNK, CHUNK), CHUNK)
        return jnp.dot(yt[...], a_ref[:, at], preferred_element_type=F32)

    def emit(j, total):
        at = pl.ds(pl.multiple_of(j * CHUNK, CHUNK), CHUNK)
        p[at, :] = (total / D).T.astype(BF16)

    sketch(w_ref)
    for i in range(POWER):
        bufs = [b.at[i] for b in (send_r, send_l, recv_l, recv_r)]
        chain_sum(me, n, chunks, part, compute, emit, bufs, ssem.at[i], rsem.at[i])
        sketch(p)


def power_call(n, deltas, weights):
    rows, ff = deltas.shape
    rank = weights.shape[1]
    tile = 256 if rows % 256 == 0 else 128
    chunks = ff // CHUNK
    comm = pltpu.VMEM((POWER, chunks, rank, CHUNK), BF16)
    vmem = pl.BlockSpec(memory_space=pltpu.VMEM)
    return pl.pallas_call(
        functools.partial(power_kernel, n, tile, chunks),
        out_shape=jax.ShapeDtypeStruct((rows, rank), BF16),
        in_specs=[vmem, vmem],
        out_specs=vmem,
        scratch_shapes=[
            pltpu.VMEM((rank, rows), BF16),
            pltpu.VMEM((ff, rank), BF16),
            pltpu.VMEM((chunks, rank, CHUNK), F32),
            comm, comm, comm, comm,
            pltpu.SemaphoreType.DMA((POWER, 2, chunks)),
            pltpu.SemaphoreType.DMA((POWER, 2, chunks)),
        ],
        compiler_params=pltpu.CompilerParams(
            collective_id=0, has_side_effects=True, vmem_limit_bytes=VMEM_LIMIT),
        cost_estimate=pl.CostEstimate(
            flops=2 * rows * ff * rank * 5, bytes_accessed=rows * ff * 2, transcendentals=0),
        name="power_steps",
    )(deltas, weights)


def cross_kernel(n, count, tile, chunks, a_ref, y_ref, gram_ref, cross_ref, ys_ref, yt, part, gpart,
                 gsend_r, gsend_l, grecv_l, grecv_r, send_r, send_l, recv_l, recv_r,
                 gssem, grsem, ssem, rsem, cssem, crsem, own_sem):
    me, own = lax.axis_index("fsdp"), lax.axis_index("ep")
    rows = a_ref.shape[0]
    bits = digits(count)
    greet(me, n, own, bits)

    place = pltpu.make_async_copy(y_ref, ys_ref.at[lax.div(own, 2)], own_sem)
    place.start()
    place.wait()
    gathers = cubes(own, count, ys_ref, cssem, crsem)
    stages = len(bits) - 1
    for gather in gathers:
        gather.run(0)

    def turn(i, carry):
        at = pl.ds(pl.multiple_of(i * tile, tile), tile)
        yt[:, at] = y_ref[at, :].astype(F32).T.astype(BF16)
        return carry

    lax.fori_loop(0, rows // tile, turn, 0)

    def compute(j):
        at = pl.ds(pl.multiple_of(j * CHUNK, CHUNK), CHUNK)
        return jnp.dot(yt[...], a_ref[:, at], preferred_element_type=F32)

    def emit(j, total):
        at = pl.ds(pl.multiple_of(j * CHUNK, CHUNK), CHUNK)
        cross_ref[:, at] = total

        @pl.when(j == chunks // 2 - 1)
        def _():
            for gather in gathers:
                gather.run(1)

    def gcompute():
        return jnp.dot(yt[...], y_ref[...], preferred_element_type=F32)

    def gemit(total):
        gram_ref[...] = total

    chain_sum(me, n, chunks, part, compute, emit, (send_r, send_l, recv_l, recv_r), ssem, rsem,
              (gpart, gcompute, gemit, (gsend_r, gsend_l, grecv_l, grecv_r), gssem, grsem))
    for stage in range(2, stages + 1):
        for gather in gathers:
            gather.run(stage)
    for gather in gathers:
        gather.finish()


def cross_call(n, count, deltas, y):
    rows, ff = deltas.shape
    rank = y.shape[1]
    tile = 256 if rows % 256 == 0 else 128
    chunks = ff // CHUNK
    comm = pltpu.VMEM((chunks, rank, CHUNK), BF16)
    gcomm = pltpu.VMEM((1, rank, rank), F32)
    vmem = pl.BlockSpec(memory_space=pltpu.VMEM)
    return pl.pallas_call(
        functools.partial(cross_kernel, n, count, tile, chunks),
        out_shape=(
            jax.ShapeDtypeStruct((rank, rank), F32),
            jax.ShapeDtypeStruct((rank, ff), F32),
            jax.ShapeDtypeStruct((count // 2, rows, rank), BF16),
        ),
        in_specs=[vmem, vmem],
        out_specs=(vmem, vmem, pl.BlockSpec(memory_space=pl.ANY)),
        scratch_shapes=[
            pltpu.VMEM((rank, rows), BF16),
            pltpu.VMEM((chunks, rank, CHUNK), F32),
            gcomm,
            gcomm, gcomm, gcomm, gcomm,
            comm, comm, comm, comm,
            pltpu.SemaphoreType.DMA((2, 1)),
            pltpu.SemaphoreType.DMA((2, 1)),
            pltpu.SemaphoreType.DMA((2, chunks)),
            pltpu.SemaphoreType.DMA((2, chunks)),
            pltpu.SemaphoreType.DMA((2, count // 2 - 1)),
            pltpu.SemaphoreType.DMA((2, count // 2 - 1)),
            pltpu.SemaphoreType.DMA,
        ],
        compiler_params=pltpu.CompilerParams(
            collective_id=1, has_side_effects=True, vmem_limit_bytes=VMEM_LIMIT),
        cost_estimate=pl.CostEstimate(
            flops=2 * rows * ff * rank * 20, bytes_accessed=rows * ff * 2, transcendentals=0),
        name="cross_gram",
    )(deltas, y)


def share_kernel(n, count, chosen_ref, other_ref, c_ref, yb_ref, c_out, y_out,
                 whole, piece, whole_send, whole_recv, piece_send, piece_recv, rows_z, y_send, y_recv,
                 wssem, wrsem, pssem, prsem, zssem, zrsem, bssem, brsem):
    me, own = lax.axis_index("fsdp"), lax.axis_index("ep")
    parity = lax.rem(own, 2)
    slots, rank, ff = c_out.shape
    half = ff // 2
    width = half // n
    bits = digits(count)
    stages = len(bits) - 1
    greet(me, n, own, bits)

    def beside(src, dst, index):
        return pltpu.make_async_remote_copy(
            src_ref=src, dst_ref=dst, send_sem=bssem.at[index], recv_sem=brsem.at[index],
            device_id={"ep": flip(own, [0])}, device_id_type=MESH)

    def for_partner(held, send):
        for s in range(slots):
            send[s] = held[lax.div(other_ref[s], 2)]

    def mine(held, recv, s):
        return jnp.where(lax.rem(chosen_ref[s], 2) == parity, held[lax.div(chosen_ref[s], 2)], recv[s])

    whole[lax.div(own, 2)] = c_ref[:, :half]
    piece[lax.div(own, 2)] = c_ref[:, pl.ds(pl.multiple_of(half + me * width, width), width)]
    pieces = cubes(own, count, piece, pssem, prsem)
    wholes = cubes(own, count, whole, wssem, wrsem)
    for gather in pieces + wholes:
        gather.run(0)
    for_partner(yb_ref, y_send)
    y_copy = beside(y_send, y_recv, 0)
    y_copy.start()
    for stage in range(1, stages):
        for gather in pieces + wholes:
            gather.run(stage)
    for gather in pieces:
        gather.run(stages)
    for_partner(piece, piece_send)
    piece_copy = beside(piece_send, piece_recv, 1)
    piece_copy.start()
    piece_copy.wait_recv()
    for s in range(slots):
        rows_z[me, s] = mine(piece, piece_recv, s)

    def right(block, hop):
        return pltpu.make_async_remote_copy(
            src_ref=rows_z.at[block], dst_ref=rows_z.at[block], send_sem=zssem.at[0, hop], recv_sem=zrsem.at[0, hop],
            device_id={"fsdp": jnp.minimum(me + 1, n - 1)}, device_id_type=MESH)

    def left(block, hop):
        return pltpu.make_async_remote_copy(
            src_ref=rows_z.at[block], dst_ref=rows_z.at[block], send_sem=zssem.at[1, hop], recv_sem=zrsem.at[1, hop],
            device_id={"fsdp": jnp.maximum(me - 1, 0)}, device_id_type=MESH)

    def send(hop, act):
        @pl.when((me - hop >= 0) & (me < n - 1))
        def _():
            act(right(me - hop, hop))

        @pl.when((me + hop <= n - 1) & (me > 0))
        def _():
            act(left(me + hop, hop))

    def receive(hop):
        @pl.when(me - 1 - hop >= 0)
        def _():
            right(me - 1 - hop, hop).wait_recv()

        @pl.when(me + 1 + hop <= n - 1)
        def _():
            left(me + 1 + hop, hop).wait_recv()

    send(0, lambda copy: copy.start())
    whole_copy = beside(whole_send, whole_recv, 2)
    for hop in range(n - 1):
        receive(hop)
        if hop < n - 2:
            send(hop + 1, lambda copy: copy.start())
        if hop == 0:
            for gather in wholes:
                gather.run(stages)
            for_partner(whole, whole_send)
            whole_copy.start()
    y_copy.wait_recv()
    for s in range(slots):
        y_out[s] = mine(yb_ref, y_recv, s)
    whole_copy.wait_recv()
    for s in range(slots):
        c_out[s, :, :half] = mine(whole, whole_recv, s)
        for z in range(n):
            c_out[s, :, half + z * width:half + (z + 1) * width] = rows_z[z, s]
    for gather in pieces + wholes:
        gather.finish()
    for copy in (y_copy, piece_copy, whole_copy):
        copy.wait_send()
    for hop in range(n - 1):
        send(hop, lambda copy: copy.wait_send())


def share_call(n, count, chosen, other, coeffs, held):
    rank, ff = coeffs.shape
    rows = held.shape[1]
    slots = chosen.shape[0]
    half, width = ff // 2, ff // 2 // n
    vmem = pl.BlockSpec(memory_space=pltpu.VMEM)
    smem = pl.BlockSpec(memory_space=pltpu.SMEM)
    dma = pltpu.SemaphoreType.DMA
    return pl.pallas_call(
        functools.partial(share_kernel, n, count),
        out_shape=(
            jax.ShapeDtypeStruct((slots, rank, ff), BF16),
            jax.ShapeDtypeStruct((slots, rows, rank), BF16),
        ),
        in_specs=[smem, smem, vmem, vmem],
        out_specs=(vmem, vmem),
        scratch_shapes=[
            pltpu.VMEM((count // 2, rank, half), BF16),
            pltpu.VMEM((count // 2, rank, width), BF16),
            pltpu.VMEM((slots, rank, half), BF16),
            pltpu.VMEM((slots, rank, half), BF16),
            pltpu.VMEM((slots, rank, width), BF16),
            pltpu.VMEM((slots, rank, width), BF16),
            pltpu.VMEM((n, slots, rank, width), BF16),
            pltpu.VMEM((slots, rows, rank), BF16),
            pltpu.VMEM((slots, rows, rank), BF16),
            dma((2, count // 2 - 1)), dma((2, count // 2 - 1)),
            dma((2, count // 2 - 1)), dma((2, count // 2 - 1)),
            dma((2, n - 1)), dma((2, n - 1)),
            dma((3,)), dma((3,)),
        ],
        compiler_params=pltpu.CompilerParams(
            collective_id=2, has_side_effects=True, vmem_limit_bytes=VMEM_LIMIT),
        name="share_chosen",
    )(chosen, other, coeffs, held)


def mul(a, b):
    return jnp.dot(a, b, preferred_element_type=F32, precision=lax.Precision.HIGHEST)


def solve_kernel(gram_ref, cross_ref, out_ref, g_ref, x_ref):
    gram = gram_ref[...]
    rank = gram.shape[0]
    eye = lax.broadcasted_iota(jnp.int32, gram.shape, 0) == lax.broadcasted_iota(jnp.int32, gram.shape, 1)
    one = jnp.where(eye, F32(1), F32(0))
    diag = jnp.where(eye, gram, F32(0))
    down = lax.rsqrt(jnp.sum(diag, axis=1, keepdims=True))
    across = lax.rsqrt(jnp.sum(diag, axis=0, keepdims=True))
    g = gram * down * across
    g_ref[...] = g
    x_ref[...] = one / jnp.max(jnp.sum(jnp.abs(g), axis=1))

    def going(carry):
        count, left = carry
        return (count < 64) & (left > 1e-6)

    def newton(carry):
        count, _ = carry
        x = x_ref[...]
        miss = one - mul(g_ref[...], x)
        x_ref[...] = x + mul(x, miss)
        return count + 1, jnp.sum(miss * miss)

    lax.while_loop(going, newton, (jnp.int32(0), F32(1e9)))
    out_ref[...] = (mul(x_ref[...], cross_ref[...] * down) * down).astype(BF16)


def solve_call(gram, cross):
    vmem = pl.BlockSpec(memory_space=pltpu.VMEM)
    return pl.pallas_call(
        solve_kernel,
        out_shape=jax.ShapeDtypeStruct(cross.shape, BF16),
        in_specs=[vmem, vmem],
        out_specs=vmem,
        scratch_shapes=[pltpu.VMEM(gram.shape, F32), pltpu.VMEM(gram.shape, F32)],
        compiler_params=pltpu.CompilerParams(vmem_limit_bytes=VMEM_LIMIT),
        cost_estimate=pl.CostEstimate(flops=10 * 10**9, bytes_accessed=10**6, transcendentals=0),
        name="solve",
    )(gram, cross)


def update_kernel(present_ref, y_ref, c_ref, serving_ref, out_ref):
    y = jnp.where(present_ref[pl.program_id(0)] == 1, y_ref[0].astype(F32), F32(0)).astype(BF16)
    update = jnp.dot(y, c_ref[0], preferred_element_type=F32)
    out_ref[0] = (serving_ref[0].astype(F32) + update).astype(BF16)


def update_call(present, ys, coeffs, serving):
    slots, rows, ff = serving.shape
    rank = ys.shape[2]
    tile = rows // 4
    return pl.pallas_call(
        update_kernel,
        out_shape=jax.ShapeDtypeStruct(serving.shape, BF16),
        grid_spec=pltpu.PrefetchScalarGridSpec(
            num_scalar_prefetch=1,
            grid=(slots, rows // tile),
            in_specs=[
                pl.BlockSpec((1, tile, rank), lambda s, i, p: (s, i, 0)),
                pl.BlockSpec((1, rank, ff), lambda s, i, p: (s, 0, 0)),
                pl.BlockSpec((1, tile, ff), lambda s, i, p: (s, i, 0)),
            ],
            out_specs=pl.BlockSpec((1, tile, ff), lambda s, i, p: (s, i, 0)),
        ),
        compiler_params=pltpu.CompilerParams(vmem_limit_bytes=VMEM_LIMIT),
        cost_estimate=pl.CostEstimate(
            flops=2 * slots * rows * ff * rank, bytes_accessed=4 * slots * rows * ff, transcendentals=0),
        name="update",
    )(present, ys, coeffs, serving)


def local(n, count, deltas, sketch_matrix, owner_of, serving):
    slot_count = serving.shape[0]
    own_index = lax.axis_index("ep")
    delta_rows = deltas[0]

    def slots_of(owner):
        is_owned = (owner_of == owner).astype(jnp.int32)
        owned_rank = jnp.cumsum(is_owned, dtype=jnp.int32) - 1
        slot_ids = jnp.arange(slot_count, dtype=jnp.int32)
        hits = (is_owned[None, :] == 1) & (owned_rank[None, :] == slot_ids[:, None])
        expert_ids = jnp.arange(owner_of.shape[0], dtype=jnp.int32)
        chosen = jnp.sum(jnp.where(hits, expert_ids[None, :], 0), axis=1).astype(jnp.int32)
        return chosen, jnp.any(hits, axis=1).astype(jnp.int32)

    chosen, present = slots_of(own_index)
    other, _ = slots_of(flip(own_index, [0]))

    y = power_call(n, delta_rows, sketch_matrix)
    gram, cross, held = cross_call(n, count, delta_rows, y)
    coeffs, ys = share_call(n, count, chosen, other, solve_call(gram, cross), held)
    return update_call(present, ys, coeffs, serving)


def solution(mesh):
    return jax.shard_map(
        functools.partial(local, mesh.shape["fsdp"], mesh.shape["ep"]),
        mesh=mesh,
        in_specs=(P("ep", "fsdp", None), P(), P(), P("ep", "fsdp", None)),
        out_specs=P("ep", "fsdp", None),
        check_vma=False,
    )
```

profile of v0, /device:TPU:0, one launch (start us, length us, event | category | flops | bytes accessed | tf_op | source)
XLA Modules:
  0.0 220.5 jit_solution(3542542349545663933)
XLA Ops:
  0.0 0.7 fusion.4
  0.7 0.2 reduce-window.17
  0.8 0.2 reduce-window.16
  1.0 0.7 fusion
  1.7 0.1 fusion.1
  1.8 0.6 convert_element_type.10.present_ref
  2.4 84.7 %power_steps.1.y_ref = bf16[1792,256]{1,0:T(8,128)(2,1)} custom-call(bf16[1792,2048]{1,0:T(8,128)(2,1)} %bitcast.9, bf16[2048,256]{1,0:T(8,128)(2,1)} %w_ref.1), custom_call_target="tpu_custom_call" | custom-call | flops 9395240960 | bytes 7340032 | tf_op jit(solution)/shard_map/power_steps/pallas_call | solution.py:250
  87.1 57.6 %cross_gram.1 = (f32[256,256]{1,0:T(8,128)}, f32[256,2048]{1,0:T(8,128)}, bf16[4,1792,256]{2,1,0:T(8,128)(2,1)}) custom-call(bf16[1792,2048]{1,0:T(8,128)(2,1)} %bitcast.10, bf16[1792,256]{1,0:T(8,128)(2,1)} %power_steps.1.y_ref), custom_call_target="tpu_custom_call" | custom-call | flops 37580963840 | bytes 7340032 | tf_op jit(solution)/shard_map/cross_gram/pallas_call | solution.py:330
  144.7 17.0 %solve.1.c_ref = bf16[256,2048]{1,0:T(8,128)(2,1)} custom-call(f32[256,256]{1,0:T(8,128)} %get-tuple-element.10.gram_ref, f32[256,2048]{1,0:T(8,128)} %get-tuple-element.11.cross_ref), custom_call_target="tpu_custom_call" | custom-call | flops 10000000000 | bytes 1000000 | tf_op jit(solution)/shard_map/solve/pallas_call | solution.py:531
  161.7 42.6 %share_chosen.1 = (bf16[2,256,2048]{2,1,0:T(8,128)(2,1)}, bf16[2,1792,256]{2,1,0:T(8,128)(2,1)}) custom-call(s32[2]{0:T(128)} %get-tuple-element.20.chosen_ref, s32[2]{0:T(128)} %get-tuple-element.19.other_ref, bf16[256,2048]{1,0:T(8,128)(2,1)} %solve.1.c_ref, bf16[4,1792,256]{2,1,0:T(8,128)(2,1)} %get-tuple-element.12.yb_ref), custom_call_target="tpu_custom_call" | custom-call | tf_op jit(solution)/shard_map/share_chosen/pallas_call | solution.py:469
  204.3 16.2 %update.1 = bf16[2,1792,2048]{2,1,0:T(8,128)(2,1)} custom-call(s32[2]{0:T(128)} %convert_element_type.10.present_ref, bf16[2,1792,256]{2,1,0:T(8,128)(2,1)} %get-tuple-element.13.y_ref, bf16[2,256,2048]{2,1,0:T(8,128)(2,1)} %get-tuple-element.14.c_ref, bf16[2,1792,2048]{2,1,0:T(8,128)(2,1)} %serving_ref.1), custom_call_target="tpu_custom_call" | custom-call | flops 3758096384 | bytes 29360128 | tf_op jit(solution)/shard_map/update/pallas_call | solution.py:553
  (2 shorter events, 0.0 us)
where the time goes:
time: 221 us; the launch traced here: 220 us
  Pallas kernels  218 us (99%)
  other arithmetic  2.42 us (1%)
    pallas_call x1, Pallas kernels, power_call(): pl.pallas_call(functools.partial(power_kernel, n, tile, chunks), out_shap...  84.7 us
    pallas_call x1, Pallas kernels, cross_call(): pl.pallas_call(functools.partial(cross_kernel, n, count, tile, chunks), o...  57.6 us
    pallas_call x1, Pallas kernels, share_call(): pl.pallas_call(functools.partial(share_kernel, n, count), out_shape=(jax....  42.6 us
    pallas_call x1, Pallas kernels, solve_call(): pl.pallas_call(solve_kernel, out_shape=jax.ShapeDtypeStruct(cross.shape,...  17 us
    pallas_call x1, Pallas kernels, update_call(): pl.pallas_call(update_kernel, out_shape=jax.ShapeDtypeStruct(serving.shap...  16.2 us

commit v1 on v0

--- a/solution.py
+++ b/solution.py
@@ -210,10 +210,13 @@
         fdrain(0, 0)
 
 
-def power_kernel(n, tile, chunks, a_ref, w_ref, y_ref, yt, p, part, send_r, send_l, recv_l, recv_r, ssem, rsem):
-    me = lax.axis_index("fsdp")
+def sketch_kernel(n, count, tile, chunks, a_ref, w_ref, gram_ref, cross_ref, ys_ref, y_ref, yt, p, part, gpart,
+                  gsend_r, gsend_l, grecv_l, grecv_r, send_r, send_l, recv_l, recv_r,
+                  gssem, grsem, ssem, rsem, cssem, crsem, own_sem):
+    me, own = lax.axis_index("fsdp"), lax.axis_index("ep")
     rows = a_ref.shape[0]
-    greet(me, n)
+    bits = digits(count)
+    greet(me, n, own, bits)
 
     def sketch(weights):
         def body(i, carry):
@@ -229,52 +232,17 @@
         at = pl.ds(pl.multiple_of(j * CHUNK, CHUNK), CHUNK)
         return jnp.dot(yt[...], a_ref[:, at], preferred_element_type=F32)
 
-    def emit(j, total):
+    def power_emit(j, total):
         at = pl.ds(pl.multiple_of(j * CHUNK, CHUNK), CHUNK)
         p[at, :] = (total / D).T.astype(BF16)
 
+    def bufs(i):
+        return [b.at[i] for b in (send_r, send_l, recv_l, recv_r)]
+
     sketch(w_ref)
     for i in range(POWER):
-        bufs = [b.at[i] for b in (send_r, send_l, recv_l, recv_r)]
-        chain_sum(me, n, chunks, part, compute, emit, bufs, ssem.at[i], rsem.at[i])
+        chain_sum(me, n, chunks, part, compute, power_emit, bufs(i), ssem.at[i], rsem.at[i])
         sketch(p)
-
-
-def power_call(n, deltas, weights):
-    rows, ff = deltas.shape
-    rank = weights.shape[1]
-    tile = 256 if rows % 256 == 0 else 128
-    chunks = ff // CHUNK
-    comm = pltpu.VMEM((POWER, chunks, rank, CHUNK), BF16)
-    vmem = pl.BlockSpec(memory_space=pltpu.VMEM)
-    return pl.pallas_call(
-        functools.partial(power_kernel, n, tile, chunks),
-        out_shape=jax.ShapeDtypeStruct((rows, rank), BF16),
-        in_specs=[vmem, vmem],
-        out_specs=vmem,
-        scratch_shapes=[
-            pltpu.VMEM((rank, rows), BF16),
-            pltpu.VMEM((ff, rank), BF16),
-            pltpu.VMEM((chunks, rank, CHUNK), F32),
-            comm, comm, comm, comm,
-            pltpu.SemaphoreType.DMA((POWER, 2, chunks)),
-            pltpu.SemaphoreType.DMA((POWER, 2, chunks)),
-        ],
-        compiler_params=pltpu.CompilerParams(
-            collective_id=0, has_side_effects=True, vmem_limit_bytes=VMEM_LIMIT),
-        cost_estimate=pl.CostEstimate(
-            flops=2 * rows * ff * rank * 5, bytes_accessed=rows * ff * 2, transcendentals=0),
-        name="power_steps",
-    )(deltas, weights)
-
-
-def cross_kernel(n, count, tile, chunks, a_ref, y_ref, gram_ref, cross_ref, ys_ref, yt, part, gpart,
-                 gsend_r, gsend_l, grecv_l, grecv_r, send_r, send_l, recv_l, recv_r,
-                 gssem, grsem, ssem, rsem, cssem, crsem, own_sem):
-    me, own = lax.axis_index("fsdp"), lax.axis_index("ep")
-    rows = a_ref.shape[0]
-    bits = digits(count)
-    greet(me, n, own, bits)
 
     place = pltpu.make_async_copy(y_ref, ys_ref.at[lax.div(own, 2)], own_sem)
     place.start()
@@ -284,22 +252,11 @@
     for gather in gathers:
         gather.run(0)
 
-    def turn(i, carry):
-        at = pl.ds(pl.multiple_of(i * tile, tile), tile)
-        yt[:, at] = y_ref[at, :].astype(F32).T.astype(BF16)
-        return carry
-
-    lax.fori_loop(0, rows // tile, turn, 0)
-
-    def compute(j):
-        at = pl.ds(pl.multiple_of(j * CHUNK, CHUNK), CHUNK)
-        return jnp.dot(yt[...], a_ref[:, at], preferred_element_type=F32)
-
-    def emit(j, total):
+    def cross_emit(j, total):
         at = pl.ds(pl.multiple_of(j * CHUNK, CHUNK), CHUNK)
         cross_ref[:, at] = total
 
-        @pl.when(j == chunks // 2 - 1)
+        @pl.when(j == chunks // 4)
         def _():
             for gather in gathers:
                 gather.run(1)
@@ -310,7 +267,7 @@
     def gemit(total):
         gram_ref[...] = total
 
-    chain_sum(me, n, chunks, part, compute, emit, (send_r, send_l, recv_l, recv_r), ssem, rsem,
+    chain_sum(me, n, chunks, part, compute, cross_emit, bufs(POWER), ssem.at[POWER], rsem.at[POWER],
               (gpart, gcompute, gemit, (gsend_r, gsend_l, grecv_l, grecv_r), gssem, grsem))
     for stage in range(2, stages + 1):
         for gather in gathers:
@@ -319,16 +276,17 @@
         gather.finish()
 
 
-def cross_call(n, count, deltas, y):
+def sketch_call(n, count, deltas, weights):
     rows, ff = deltas.shape
-    rank = y.shape[1]
+    rank = weights.shape[1]
     tile = 256 if rows % 256 == 0 else 128
     chunks = ff // CHUNK
-    comm = pltpu.VMEM((chunks, rank, CHUNK), BF16)
+    comm = pltpu.VMEM((POWER + 1, chunks, rank, CHUNK), BF16)
     gcomm = pltpu.VMEM((1, rank, rank), F32)
     vmem = pl.BlockSpec(memory_space=pltpu.VMEM)
+    dma = pltpu.SemaphoreType.DMA
     return pl.pallas_call(
-        functools.partial(cross_kernel, n, count, tile, chunks),
+        functools.partial(sketch_kernel, n, count, tile, chunks),
         out_shape=(
             jax.ShapeDtypeStruct((rank, rank), F32),
             jax.ShapeDtypeStruct((rank, ff), F32),
@@ -337,25 +295,24 @@
         in_specs=[vmem, vmem],
         out_specs=(vmem, vmem, pl.BlockSpec(memory_space=pl.ANY)),
         scratch_shapes=[
+            pltpu.VMEM((rows, rank), BF16),
             pltpu.VMEM((rank, rows), BF16),
+            pltpu.VMEM((ff, rank), BF16),
             pltpu.VMEM((chunks, rank, CHUNK), F32),
             gcomm,
             gcomm, gcomm, gcomm, gcomm,
             comm, comm, comm, comm,
-            pltpu.SemaphoreType.DMA((2, 1)),
-            pltpu.SemaphoreType.DMA((2, 1)),
-            pltpu.SemaphoreType.DMA((2, chunks)),
-            pltpu.SemaphoreType.DMA((2, chunks)),
-            pltpu.SemaphoreType.DMA((2, count // 2 - 1)),
-            pltpu.SemaphoreType.DMA((2, count // 2 - 1)),
-            pltpu.SemaphoreType.DMA,
+            dma((2, 1)), dma((2, 1)),
+            dma((POWER + 1, 2, chunks)), dma((POWER + 1, 2, chunks)),
+            dma((2, count // 2 - 1)), dma((2, count // 2 - 1)),
+            dma,
         ],
         compiler_params=pltpu.CompilerParams(
-            collective_id=1, has_side_effects=True, vmem_limit_bytes=VMEM_LIMIT),
+            collective_id=0, has_side_effects=True, vmem_limit_bytes=VMEM_LIMIT),
         cost_estimate=pl.CostEstimate(
-            flops=2 * rows * ff * rank * 20, bytes_accessed=rows * ff * 2, transcendentals=0),
-        name="cross_gram",
-    )(deltas, y)
+            flops=2 * rows * ff * rank * 6, bytes_accessed=rows * ff * 2, transcendentals=0),
+        name="sketch_sums",
+    )(deltas, weights)
 
 
 def share_kernel(n, count, chosen_ref, other_ref, c_ref, yb_ref, c_out, y_out,
@@ -389,8 +346,8 @@
     for gather in pieces + wholes:
         gather.run(0)
     for_partner(yb_ref, y_send)
-    y_copy = beside(y_send, y_recv, 0)
-    y_copy.start()
+    y_copies = [beside(y_send.at[s], y_recv.at[s], 2 + s) for s in range(slots)]
+    y_copies[0].start()
     for stage in range(1, stages):
         for gather in pieces + wholes:
             gather.run(stage)
@@ -432,7 +389,9 @@
             left(me + 1 + hop, hop).wait_recv()
 
     send(0, lambda copy: copy.start())
-    whole_copy = beside(whole_send, whole_recv, 2)
+    for copy in y_copies[1:]:
+        copy.start()
+    whole_copy = beside(whole_send, whole_recv, 0)
     for hop in range(n - 1):
         receive(hop)
         if hop < n - 2:
@@ -442,8 +401,8 @@
                 gather.run(stages)
             for_partner(whole, whole_send)
             whole_copy.start()
-    y_copy.wait_recv()
     for s in range(slots):
+        y_copies[s].wait_recv()
         y_out[s] = mine(yb_ref, y_recv, s)
     whole_copy.wait_recv()
     for s in range(slots):
@@ -452,7 +411,7 @@
             c_out[s, :, half + z * width:half + (z + 1) * width] = rows_z[z, s]
     for gather in pieces + wholes:
         gather.finish()
-    for copy in (y_copy, piece_copy, whole_copy):
+    for copy in y_copies + [piece_copy, whole_copy]:
         copy.wait_send()
     for hop in range(n - 1):
         send(hop, lambda copy: copy.wait_send())
@@ -487,10 +446,10 @@
             dma((2, count // 2 - 1)), dma((2, count // 2 - 1)),
             dma((2, count // 2 - 1)), dma((2, count // 2 - 1)),
             dma((2, n - 1)), dma((2, n - 1)),
-            dma((3,)), dma((3,)),
+            dma((2 + slots,)), dma((2 + slots,)),
         ],
         compiler_params=pltpu.CompilerParams(
-            collective_id=2, has_side_effects=True, vmem_limit_bytes=VMEM_LIMIT),
+            collective_id=1, has_side_effects=True, vmem_limit_bytes=VMEM_LIMIT),
         name="share_chosen",
     )(chosen, other, coeffs, held)
 
@@ -509,11 +468,24 @@
     across = lax.rsqrt(jnp.sum(diag, axis=0, keepdims=True))
     g = gram * down * across
     g_ref[...] = g
-    x_ref[...] = one / jnp.max(jnp.sum(jnp.abs(g), axis=1))
-
-    def going(carry):
-        count, left = carry
-        return (count < 64) & (left > 1e-6)
+    start = one / jnp.max(jnp.sum(jnp.abs(g), axis=1))
+    x_ref[...] = start
+
+    def rough(carry):
+        count, _ = carry
+        x = x_ref[...]
+        low = x.astype(BF16)
+        miss = one - jnp.dot(g_ref[...].astype(BF16), low, preferred_element_type=F32)
+        x_ref[...] = x + jnp.dot(low, miss.astype(BF16), preferred_element_type=F32)
+        return count + 1, jnp.sum(miss * miss)
+
+    lax.while_loop(lambda c: (c[0] < 16) & (c[1] > 0.3), rough, (jnp.int32(0), F32(1e9)))
+    miss = one - mul(g_ref[...], x_ref[...])
+    sound = jnp.sum(miss * miss) < 0.9
+
+    @pl.when(jnp.logical_not(sound))
+    def _():
+        x_ref[...] = start
 
     def newton(carry):
         count, _ = carry
@@ -522,7 +494,7 @@
         x_ref[...] = x + mul(x, miss)
         return count + 1, jnp.sum(miss * miss)
 
-    lax.while_loop(going, newton, (jnp.int32(0), F32(1e9)))
+    lax.while_loop(lambda c: (c[0] < 64) & (c[1] > 1e-6), newton, (jnp.int32(0), F32(1e9)))
     out_ref[...] = (mul(x_ref[...], cross_ref[...] * down) * down).astype(BF16)
 
 
@@ -542,8 +514,13 @@
 
 def update_kernel(present_ref, y_ref, c_ref, serving_ref, out_ref):
     y = jnp.where(present_ref[pl.program_id(0)] == 1, y_ref[0].astype(F32), F32(0)).astype(BF16)
-    update = jnp.dot(y, c_ref[0], preferred_element_type=F32)
-    out_ref[0] = (serving_ref[0].astype(F32) + update).astype(BF16)
+    tile, ff = y.shape[0], c_ref.shape[2]
+    for at in range(0, ff, 256):
+        columns = slice(at, at + 256)
+        for top in range(0, tile, tile // 2):
+            rows = slice(top, top + tile // 2)
+            update = jnp.dot(y[rows], c_ref[0, :, columns], preferred_element_type=F32)
+            out_ref[0, rows, columns] = (serving_ref[0, rows, columns].astype(F32) + update).astype(BF16)
 
 
 def update_call(present, ys, coeffs, serving):
@@ -587,8 +564,7 @@
     chosen, present = slots_of(own_index)
     other, _ = slots_of(flip(own_index, [0]))
 
-    y = power_call(n, delta_rows, sketch_matrix)
-    gram, cross, held = cross_call(n, count, delta_rows, y)
+    gram, cross, held = sketch_call(n, count, delta_rows, sketch_matrix)
     coeffs, ys = share_call(n, count, chosen, other, solve_call(gram, cross), held)
     return update_call(present, ys, coeffs, serving)
 

time: 221 us -> 202 us (0.914)
  Pallas kernels: 218 us -> 199 us
    pallas_call x2 -> x1, Pallas kernels: 142 us -> 130 us  [sketch_call(): pl.pallas_call(functools.partial(sketch_kernel, n, count, tile, chunks),...]
    pallas_call x1, Pallas kernels: 17 us -> 11.2 us  [solve_call(): pl.pallas_call(solve_kernel, out_shape=jax.ShapeDtypeStruct(cross.shape,...]
where the time goes in v1:
time: 202 us
  Pallas kernels  199 us (99%)
  other arithmetic  2.42 us (1%)
    pallas_call x1, Pallas kernels, sketch_call(): pl.pallas_call(functools.partial(sketch_kernel, n, count, tile, chunks),...  130 us
    pallas_call x1, Pallas kernels, share_call(): pl.pallas_call(functools.partial(share_kernel, n, count), out_shape=(jax....  41.7 us
    pallas_call x1, Pallas kernels, update_call(): pl.pallas_call(update_kernel, out_shape=jax.ShapeDtypeStruct(serving.shap...  16.2 us
    pallas_call x1, Pallas kernels, solve_call(): pl.pallas_call(solve_kernel, out_shape=jax.ShapeDtypeStruct(cross.shape,...  11.2 us

profile of v1, /device:TPU:0, one launch (start us, length us, event | category | flops | bytes accessed | tf_op | source)
XLA Modules:
  0.0 201.8 jit_solution(4332145740437285207)
XLA Ops:
  0.0 0.7 fusion.4
  0.7 0.2 reduce-window.17
  0.8 0.2 reduce-window.16
  1.0 0.7 fusion
  1.7 0.1 fusion.1
  1.8 0.6 convert_element_type.10.present_ref
  2.4 130.2 %sketch_sums.1 = (f32[256,256]{1,0:T(8,128)}, f32[256,2048]{1,0:T(8,128)}, bf16[4,1792,256]{2,1,0:T(8,128)(2,1)}) custom-call(bf16[1792,2048]{1,0:T(8,128)(2,1)} %bitcast.9, bf16[2048,256]{1,0:T(8,128)(2,1)} %w_ref.1), custom_call_target="tpu_custom_call" | custom-call | flops 11274289152 | bytes 7340032 | tf_op jit(solution)/shard_map/sketch_sums/pallas_call | solution.py:288
  132.7 11.2 %solve.1.c_ref = bf16[256,2048]{1,0:T(8,128)(2,1)} custom-call(f32[256,256]{1,0:T(8,128)} %get-tuple-element.10.gram_ref, f32[256,2048]{1,0:T(8,128)} %get-tuple-element.11.cross_ref), custom_call_target="tpu_custom_call" | custom-call | flops 10000000000 | bytes 1000000 | tf_op jit(solution)/shard_map/solve/pallas_call | solution.py:503
  143.9 41.7 %share_chosen.1 = (bf16[2,256,2048]{2,1,0:T(8,128)(2,1)}, bf16[2,1792,256]{2,1,0:T(8,128)(2,1)}) custom-call(s32[2]{0:T(128)} %get-tuple-element.20.chosen_ref, s32[2]{0:T(128)} %get-tuple-element.19.other_ref, bf16[256,2048]{1,0:T(8,128)(2,1)} %solve.1.c_ref, bf16[4,1792,256]{2,1,0:T(8,128)(2,1)} %get-tuple-element.12.yb_ref), custom_call_target="tpu_custom_call" | custom-call | tf_op jit(solution)/shard_map/share_chosen/pallas_call | solution.py:428
  185.6 16.2 %update.1 = bf16[2,1792,2048]{2,1,0:T(8,128)(2,1)} custom-call(s32[2]{0:T(128)} %convert_element_type.10.present_ref, bf16[2,1792,256]{2,1,0:T(8,128)(2,1)} %get-tuple-element.13.y_ref, bf16[2,256,2048]{2,1,0:T(8,128)(2,1)} %get-tuple-element.14.c_ref, bf16[2,1792,2048]{2,1,0:T(8,128)(2,1)} %serving_ref.1), custom_call_target="tpu_custom_call" | custom-call | flops 3758096384 | bytes 29360128 | tf_op jit(solution)/shard_map/update/pallas_call | solution.py:530
  (2 shorter events, 0.0 us)

commit v2 on v1

--- a/solution.py
+++ b/solution.py
@@ -11,6 +11,7 @@
 POWER = 2
 MESH = pl.DeviceIdType.MESH
 CHUNK = 128
+PIECES = 4
 VMEM_LIMIT = 56 * 1024 * 1024
 F32 = jnp.float32
 BF16 = jnp.bfloat16
@@ -147,33 +148,36 @@
     rightward, leftward, total, drain = moves(me, n, part, bufs, ssem, rsem)
     if first is not None:
         fpart, fcompute, femit, fbufs, fssem, frsem = first
+        pieces = fpart.shape[0]
         frightward, fleftward, ftotal, fdrain = moves(me, n, fpart, fbufs, fssem, frsem)
 
     def step(t, carry):
         if first is not None:
-            @pl.when(t == 0)
+            @pl.when(t < pieces)
             def _():
-                fpart[0] = fcompute()
+                fpart[t] = fcompute(t)
 
                 @pl.when(lower)
                 def _():
-                    frightward(0)
+                    frightward(t)
 
                 @pl.when(jnp.logical_not(lower))
                 def _():
-                    fleftward(0)
-
-            @pl.when(t == skew)
+                    fleftward(t)
+
+            @pl.when((t >= skew) & (t < skew + pieces))
             def _():
+                i = t - skew
+
                 @pl.when(lower)
                 def _():
-                    fleftward(0)
+                    fleftward(i)
 
                 @pl.when(jnp.logical_not(lower))
                 def _():
-                    frightward(0)
-
-                femit(ftotal(0))
+                    frightward(i)
+
+                femit(i, ftotal(i))
 
         @pl.when(t < chunks)
         def _():
@@ -207,20 +211,32 @@
 
     lax.fori_loop(0, chunks, drain, 0)
     if first is not None:
-        fdrain(0, 0)
-
-
-def sketch_kernel(n, count, tile, chunks, a_ref, w_ref, gram_ref, cross_ref, ys_ref, y_ref, yt, p, part, gpart,
+        lax.fori_loop(0, pieces, fdrain, 0)
+
+
+def sketch_kernel(n, count, tile, chunks, a_hbm, w_ref, gram_ref, cross_ref, ys_ref, a_ref, a_sem, y_ref, yt, p, part, gpart,
                   gsend_r, gsend_l, grecv_l, grecv_r, send_r, send_l, recv_l, recv_r,
                   gssem, grsem, ssem, rsem, cssem, crsem, own_sem):
     me, own = lax.axis_index("fsdp"), lax.axis_index("ep")
     rows = a_ref.shape[0]
     bits = digits(count)
+
+    def load(i):
+        at = pl.ds(pl.multiple_of(i * tile, tile), tile)
+        return pltpu.make_async_copy(a_hbm.at[at], a_ref.at[at], a_sem.at[i])
+
+    def begin(i, carry):
+        load(i).start()
+        return carry
+
+    lax.fori_loop(0, rows // tile, begin, 0)
     greet(me, n, own, bits)
 
-    def sketch(weights):
+    def sketch(weights, loading=False):
         def body(i, carry):
             at = pl.ds(pl.multiple_of(i * tile, tile), tile)
+            if loading:
+                load(i).wait()
             block = jnp.dot(a_ref[at, :], weights[...], preferred_element_type=F32)
             y_ref[at, :] = block.astype(BF16)
             yt[:, at] = block.T.astype(BF16)
@@ -239,7 +255,7 @@
     def bufs(i):
         return [b.at[i] for b in (send_r, send_l, recv_l, recv_r)]
 
-    sketch(w_ref)
+    sketch(w_ref, True)
     for i in range(POWER):
         chain_sum(me, n, chunks, part, compute, power_emit, bufs(i), ssem.at[i], rsem.at[i])
         sketch(p)
@@ -256,16 +272,21 @@
         at = pl.ds(pl.multiple_of(j * CHUNK, CHUNK), CHUNK)
         cross_ref[:, at] = total
 
-        @pl.when(j == chunks // 4)
+        edge = (me == 0) | (me == n - 1)
+
+        @pl.when(j == jnp.where(edge, 0, chunks // 4))
         def _():
             for gather in gathers:
                 gather.run(1)
 
-    def gcompute():
-        return jnp.dot(yt[...], y_ref[...], preferred_element_type=F32)
-
-    def gemit(total):
-        gram_ref[...] = total
+    band = gpart.shape[1]
+
+    def gcompute(i):
+        at = pl.ds(pl.multiple_of(i * band, band), band)
+        return jnp.dot(yt[at, :], y_ref[...], preferred_element_type=F32)
+
+    def gemit(i, total):
+        gram_ref[pl.ds(pl.multiple_of(i * band, band), band), :] = total
 
     chain_sum(me, n, chunks, part, compute, cross_emit, bufs(POWER), ssem.at[POWER], rsem.at[POWER],
               (gpart, gcompute, gemit, (gsend_r, gsend_l, grecv_l, grecv_r), gssem, grsem))
@@ -282,7 +303,7 @@
     tile = 256 if rows % 256 == 0 else 128
     chunks = ff // CHUNK
     comm = pltpu.VMEM((POWER + 1, chunks, rank, CHUNK), BF16)
-    gcomm = pltpu.VMEM((1, rank, rank), F32)
+    gcomm = pltpu.VMEM((PIECES, rank // PIECES, rank), F32)
     vmem = pl.BlockSpec(memory_space=pltpu.VMEM)
     dma = pltpu.SemaphoreType.DMA
     return pl.pallas_call(
@@ -292,9 +313,11 @@
             jax.ShapeDtypeStruct((rank, ff), F32),
             jax.ShapeDtypeStruct((count // 2, rows, rank), BF16),
         ),
-        in_specs=[vmem, vmem],
+        in_specs=[pl.BlockSpec(memory_space=pl.ANY), vmem],
         out_specs=(vmem, vmem, pl.BlockSpec(memory_space=pl.ANY)),
         scratch_shapes=[
+            pltpu.VMEM((rows, ff), BF16),
+            dma((rows // tile,)),
             pltpu.VMEM((rows, rank), BF16),
             pltpu.VMEM((rank, rows), BF16),
             pltpu.VMEM((ff, rank), BF16),
@@ -302,7 +325,7 @@
             gcomm,
             gcomm, gcomm, gcomm, gcomm,
             comm, comm, comm, comm,
-            dma((2, 1)), dma((2, 1)),
+            dma((2, PIECES)), dma((2, PIECES)),
             dma((POWER + 1, 2, chunks)), dma((POWER + 1, 2, chunks)),
             dma((2, count // 2 - 1)), dma((2, count // 2 - 1)),
             dma,
@@ -315,7 +338,7 @@
     )(deltas, weights)
 
 
-def share_kernel(n, count, chosen_ref, other_ref, c_ref, yb_ref, c_out, y_out,
+def share_kernel(n, count, owner_ref, c_ref, yb_ref, c_out, y_out,
                  whole, piece, whole_send, whole_recv, piece_send, piece_recv, rows_z, y_send, y_recv,
                  wssem, wrsem, pssem, prsem, zssem, zrsem, bssem, brsem):
     me, own = lax.axis_index("fsdp"), lax.axis_index("ep")
@@ -327,6 +350,20 @@
     stages = len(bits) - 1
     greet(me, n, own, bits)
 
+    def slots_of(owner):
+        seen, chosen, present = jnp.int32(0), [jnp.int32(0)] * slots, [jnp.int32(0)] * slots
+        for expert in range(count):
+            owned = (owner_ref[expert] == owner).astype(jnp.int32)
+            for s in range(slots):
+                hit = owned * (seen == s).astype(jnp.int32)
+                chosen[s] = chosen[s] + hit * expert
+                present[s] = present[s] + hit
+            seen = seen + owned
+        return chosen, present
+
+    chosen, present = slots_of(own)
+    other, _ = slots_of(flip(own, [0]))
+
     def beside(src, dst, index):
         return pltpu.make_async_remote_copy(
             src_ref=src, dst_ref=dst, send_sem=bssem.at[index], recv_sem=brsem.at[index],
@@ -334,28 +371,33 @@
 
     def for_partner(held, send):
         for s in range(slots):
-            send[s] = held[lax.div(other_ref[s], 2)]
+            send[s] = held[lax.div(other[s], 2)]
 
     def mine(held, recv, s):
-        return jnp.where(lax.rem(chosen_ref[s], 2) == parity, held[lax.div(chosen_ref[s], 2)], recv[s])
+        return jnp.where(lax.rem(chosen[s], 2) == parity, held[lax.div(chosen[s], 2)], recv[s])
 
     whole[lax.div(own, 2)] = c_ref[:, :half]
     piece[lax.div(own, 2)] = c_ref[:, pl.ds(pl.multiple_of(half + me * width, width), width)]
     pieces = cubes(own, count, piece, pssem, prsem)
     wholes = cubes(own, count, whole, wssem, wrsem)
-    for gather in pieces + wholes:
+    for gather in pieces:
+        gather.run(0)
+    for gather in pieces:
+        gather.run(1)
+    for gather in wholes:
         gather.run(0)
     for_partner(yb_ref, y_send)
     y_copies = [beside(y_send.at[s], y_recv.at[s], 2 + s) for s in range(slots)]
     y_copies[0].start()
-    for stage in range(1, stages):
-        for gather in pieces + wholes:
+    for stage in range(2, stages + 1):
+        for gather in pieces:
             gather.run(stage)
-    for gather in pieces:
-        gather.run(stages)
     for_partner(piece, piece_send)
     piece_copy = beside(piece_send, piece_recv, 1)
     piece_copy.start()
+    for stage in range(1, stages):
+        for gather in wholes:
+            gather.run(stage)
     piece_copy.wait_recv()
     for s in range(slots):
         rows_z[me, s] = mine(piece, piece_recv, s)
@@ -403,7 +445,7 @@
             whole_copy.start()
     for s in range(slots):
         y_copies[s].wait_recv()
-        y_out[s] = mine(yb_ref, y_recv, s)
+        y_out[s] = jnp.where(present[s] == 1, mine(yb_ref, y_recv, s), jnp.zeros_like(y_recv[s]))
     whole_copy.wait_recv()
     for s in range(slots):
         c_out[s, :, :half] = mine(whole, whole_recv, s)
@@ -417,10 +459,9 @@
         send(hop, lambda copy: copy.wait_send())
 
 
-def share_call(n, count, chosen, other, coeffs, held):
+def share_call(n, count, slots, owner_of, coeffs, held):
     rank, ff = coeffs.shape
     rows = held.shape[1]
-    slots = chosen.shape[0]
     half, width = ff // 2, ff // 2 // n
     vmem = pl.BlockSpec(memory_space=pltpu.VMEM)
     smem = pl.BlockSpec(memory_space=pltpu.SMEM)
@@ -431,7 +472,7 @@
             jax.ShapeDtypeStruct((slots, rank, ff), BF16),
             jax.ShapeDtypeStruct((slots, rows, rank), BF16),
         ),
-        in_specs=[smem, smem, vmem, vmem],
+        in_specs=[smem, vmem, vmem],
         out_specs=(vmem, vmem),
         scratch_shapes=[
             pltpu.VMEM((count // 2, rank, half), BF16),
@@ -451,7 +492,7 @@
         compiler_params=pltpu.CompilerParams(
             collective_id=1, has_side_effects=True, vmem_limit_bytes=VMEM_LIMIT),
         name="share_chosen",
-    )(chosen, other, coeffs, held)
+    )(owner_of, coeffs, held)
 
 
 def mul(a, b):
@@ -512,61 +553,41 @@
     )(gram, cross)
 
 
-def update_kernel(present_ref, y_ref, c_ref, serving_ref, out_ref):
-    y = jnp.where(present_ref[pl.program_id(0)] == 1, y_ref[0].astype(F32), F32(0)).astype(BF16)
-    tile, ff = y.shape[0], c_ref.shape[2]
+def update_kernel(y_ref, c_ref, serving_ref, out_ref):
+    tile, ff = y_ref.shape[1], c_ref.shape[2]
     for at in range(0, ff, 256):
         columns = slice(at, at + 256)
         for top in range(0, tile, tile // 2):
             rows = slice(top, top + tile // 2)
-            update = jnp.dot(y[rows], c_ref[0, :, columns], preferred_element_type=F32)
+            update = jnp.dot(y_ref[0, rows, :], c_ref[0, :, columns], preferred_element_type=F32)
             out_ref[0, rows, columns] = (serving_ref[0, rows, columns].astype(F32) + update).astype(BF16)
 
 
-def update_call(present, ys, coeffs, serving):
+def update_call(ys, coeffs, serving):
     slots, rows, ff = serving.shape
     rank = ys.shape[2]
-    tile = rows // 4
+    tile = rows // 2
     return pl.pallas_call(
         update_kernel,
         out_shape=jax.ShapeDtypeStruct(serving.shape, BF16),
-        grid_spec=pltpu.PrefetchScalarGridSpec(
-            num_scalar_prefetch=1,
-            grid=(slots, rows // tile),
-            in_specs=[
-                pl.BlockSpec((1, tile, rank), lambda s, i, p: (s, i, 0)),
-                pl.BlockSpec((1, rank, ff), lambda s, i, p: (s, 0, 0)),
-                pl.BlockSpec((1, tile, ff), lambda s, i, p: (s, i, 0)),
-            ],
-            out_specs=pl.BlockSpec((1, tile, ff), lambda s, i, p: (s, i, 0)),
-        ),
+        grid=(slots, rows // tile),
+        in_specs=[
+            pl.BlockSpec((1, tile, rank), lambda s, i: (s, i, 0)),
+            pl.BlockSpec((1, rank, ff), lambda s, i: (s, 0, 0)),
+            pl.BlockSpec((1, tile, ff), lambda s, i: (s, i, 0)),
+        ],
+        out_specs=pl.BlockSpec((1, tile, ff), lambda s, i: (s, i, 0)),
         compiler_params=pltpu.CompilerParams(vmem_limit_bytes=VMEM_LIMIT),
         cost_estimate=pl.CostEstimate(
             flops=2 * slots * rows * ff * rank, bytes_accessed=4 * slots * rows * ff, transcendentals=0),
         name="update",
-    )(present, ys, coeffs, serving)
+    )(ys, coeffs, serving)
 
 
 def local(n, count, deltas, sketch_matrix, owner_of, serving):
-    slot_count = serving.shape[0]
-    own_index = lax.axis_index("ep")
-    delta_rows = deltas[0]
-
-    def slots_of(owner):
-        is_owned = (owner_of == owner).astype(jnp.int32)
-        owned_rank = jnp.cumsum(is_owned, dtype=jnp.int32) - 1
-        slot_ids = jnp.arange(slot_count, dtype=jnp.int32)
-        hits = (is_owned[None, :] == 1) & (owned_rank[None, :] == slot_ids[:, None])
-        expert_ids = jnp.arange(owner_of.shape[0], dtype=jnp.int32)
-        chosen = jnp.sum(jnp.where(hits, expert_ids[None, :], 0), axis=1).astype(jnp.int32)
-        return chosen, jnp.any(hits, axis=1).astype(jnp.int32)
-
-    chosen, present = slots_of(own_index)
-    other, _ = slots_of(flip(own_index, [0]))
-
-    gram, cross, held = sketch_call(n, count, delta_rows, sketch_matrix)
-    coeffs, ys = share_call(n, count, chosen, other, solve_call(gram, cross), held)
-    return update_call(present, ys, coeffs, serving)
+    gram, cross, held = sketch_call(n, count, deltas[0], sketch_matrix)
+    coeffs, ys = share_call(n, count, serving.shape[0], owner_of, solve_call(gram, cross), held)
+    return update_call(ys, coeffs, serving)
 
 
 def solution(mesh):

time: 202 us -> 186 us (0.921)
  Pallas kernels: 199 us -> 186 us
  other arithmetic: 2.42 us -> 0 us
    pallas_call x1, Pallas kernels: 130 us -> 123 us  [sketch_call(): pl.pallas_call(functools.partial(sketch_kernel, n, count, tile, chunks),...]
    pallas_call x1, Pallas kernels: 41.7 us -> 38.5 us  [share_call(): pl.pallas_call(functools.partial(share_kernel, n, count), out_shape=(jax....]
    pallas_call x1, Pallas kernels: 16.2 us -> 13 us  [update_call(): pl.pallas_call(update_kernel, out_shape=jax.ShapeDtypeStruct(serving.shap...]
where the time goes in v2:
time: 186 us
  Pallas kernels  186 us (100%)
    pallas_call x1, Pallas kernels, sketch_call(): pl.pallas_call(functools.partial(sketch_kernel, n, count, tile, chunks),...  123 us
    pallas_call x1, Pallas kernels, share_call(): pl.pallas_call(functools.partial(share_kernel, n, count), out_shape=(jax....  38.5 us
    pallas_call x1, Pallas kernels, update_call(): pl.pallas_call(update_kernel, out_shape=jax.ShapeDtypeStruct(serving.shap...  13 us
    pallas_call x1, Pallas kernels, solve_call(): pl.pallas_call(solve_kernel, out_shape=jax.ShapeDtypeStruct(cross.shape,...  11.2 us

profile of v2, /device:TPU:0, one launch (start us, length us, event | category | flops | bytes accessed | tf_op | source)
XLA Modules:
  0.0 185.9 jit_solution(8737643484040820219)
XLA Ops:
  0.0 123.1 %sketch_sums.1 = (f32[256,256]{1,0:T(8,128)}, f32[256,2048]{1,0:T(8,128)}, bf16[4,1792,256]{2,1,0:T(8,128)(2,1)}) custom-call(bf16[1792,2048]{1,0:T(8,128)(2,1)} %bitcast.1, bf16[2048,256]{1,0:T(8,128)(2,1)} %w_ref.1), custom_call_target="tpu_custom_call" | custom-call | flops 11274289152 | bytes 7340032 | tf_op jit(solution)/shard_map/sketch_sums/pallas_call | solution.py:309
  123.1 11.2 %solve.1.c_ref = bf16[256,2048]{1,0:T(8,128)(2,1)} custom-call(f32[256,256]{1,0:T(8,128)} %get-tuple-element.10.gram_ref, f32[256,2048]{1,0:T(8,128)} %get-tuple-element.11.cross_ref), custom_call_target="tpu_custom_call" | custom-call | flops 10000000000 | bytes 1000000 | tf_op jit(solution)/shard_map/solve/pallas_call | solution.py:544
  134.3 38.5 %share_chosen.1 = (bf16[2,256,2048]{2,1,0:T(8,128)(2,1)}, bf16[2,1792,256]{2,1,0:T(8,128)(2,1)}) custom-call(s32[8]{0:T(128)} %owner_ref.1, bf16[256,2048]{1,0:T(8,128)(2,1)} %solve.1.c_ref, bf16[4,1792,256]{2,1,0:T(8,128)(2,1)} %get-tuple-element.12.yb_ref), custom_call_target="tpu_custom_call" | custom-call | tf_op jit(solution)/shard_map/share_chosen/pallas_call | solution.py:469
  172.8 13.0 %update.1 = bf16[2,1792,2048]{2,1,0:T(8,128)(2,1)} custom-call(bf16[2,1792,256]{2,1,0:T(8,128)(2,1)} %get-tuple-element.13.y_ref, bf16[2,256,2048]{2,1,0:T(8,128)(2,1)} %get-tuple-element.14.c_ref, bf16[2,1792,2048]{2,1,0:T(8,128)(2,1)} %serving_ref.1), custom_call_target="tpu_custom_call" | custom-call | flops 3758096384 | bytes 29360128 | tf_op jit(solution)/shard_map/update/pallas_call | solution.py:570

commit v3 on v2

--- a/solution.py
+++ b/solution.py
@@ -144,7 +144,7 @@
 def chain_sum(me, n, chunks, part, compute, emit, bufs, ssem, rsem, first=None):
     lower = me < n // 2
     edge = jnp.minimum(me, n - 1 - me)
-    skew = jnp.where(edge == 0, chunks, jnp.minimum(n - 2 * edge, chunks))
+    skew = jnp.where(edge == 0, chunks, jnp.minimum(n + 2 - 2 * edge, chunks))
     rightward, leftward, total, drain = moves(me, n, part, bufs, ssem, rsem)
     if first is not None:
         fpart, fcompute, femit, fbufs, fssem, frsem = first

time: 186 us -> 189 us (1.016)
  Pallas kernels: 186 us -> 189 us
    pallas_call x1, Pallas kernels: 123 us -> 126 us  [sketch_call(): pl.pallas_call(functools.partial(sketch_kernel, n, count, tile, chunks),...]
where the time goes in v3:
time: 189 us
  Pallas kernels  189 us (100%)
    pallas_call x1, Pallas kernels, sketch_call(): pl.pallas_call(functools.partial(sketch_kernel, n, count, tile, chunks),...  126 us
    pallas_call x1, Pallas kernels, share_call(): pl.pallas_call(functools.partial(share_kernel, n, count), out_shape=(jax....  39.4 us
    pallas_call x1, Pallas kernels, update_call(): pl.pallas_call(update_kernel, out_shape=jax.ShapeDtypeStruct(serving.shap...  13 us
    pallas_call x1, Pallas kernels, solve_call(): pl.pallas_call(solve_kernel, out_shape=jax.ShapeDtypeStruct(cross.shape,...  11.2 us

profile of v3, /device:TPU:0, one launch (start us, length us, event | category | flops | bytes accessed | tf_op | source)
XLA Modules:
  0.0 189.3 jit_solution(14362041260614331976)
XLA Ops:
  0.0 125.6 %sketch_sums.1 = (f32[256,256]{1,0:T(8,128)}, f32[256,2048]{1,0:T(8,128)}, bf16[4,1792,256]{2,1,0:T(8,128)(2,1)}) custom-call(bf16[1792,2048]{1,0:T(8,128)(2,1)} %bitcast.1, bf16[2048,256]{1,0:T(8,128)(2,1)} %w_ref.1), custom_call_target="tpu_custom_call" | custom-call | flops 11274289152 | bytes 7340032 | tf_op jit(solution)/shard_map/sketch_sums/pallas_call | solution.py:309
  125.6 11.2 %solve.1.c_ref = bf16[256,2048]{1,0:T(8,128)(2,1)} custom-call(f32[256,256]{1,0:T(8,128)} %get-tuple-element.10.gram_ref, f32[256,2048]{1,0:T(8,128)} %get-tuple-element.11.cross_ref), custom_call_target="tpu_custom_call" | custom-call | flops 10000000000 | bytes 1000000 | tf_op jit(solution)/shard_map/solve/pallas_call | solution.py:544
  136.8 39.4 %share_chosen.1 = (bf16[2,256,2048]{2,1,0:T(8,128)(2,1)}, bf16[2,1792,256]{2,1,0:T(8,128)(2,1)}) custom-call(s32[8]{0:T(128)} %owner_ref.1, bf16[256,2048]{1,0:T(8,128)(2,1)} %solve.1.c_ref, bf16[4,1792,256]{2,1,0:T(8,128)(2,1)} %get-tuple-element.12.yb_ref), custom_call_target="tpu_custom_call" | custom-call | tf_op jit(solution)/shard_map/share_chosen/pallas_call | solution.py:469
  176.2 13.0 %update.1 = bf16[2,1792,2048]{2,1,0:T(8,128)(2,1)} custom-call(bf16[2,1792,256]{2,1,0:T(8,128)(2,1)} %get-tuple-element.13.y_ref, bf16[2,256,2048]{2,1,0:T(8,128)(2,1)} %get-tuple-element.14.c_ref, bf16[2,1792,2048]{2,1,0:T(8,128)(2,1)} %serving_ref.1), custom_call_target="tpu_custom_call" | custom-call | flops 3758096384 | bytes 29360128 | tf_op jit(solution)/shard_map/update/pallas_call | solution.py:570
